TPU v7x, 128 devices: a whole 4x4x4 slice. The times are simulated.
128 devices in a mesh: dp: 32 (over x, y, core), fsdp: 4 (over z).
Axes of the slice: x: 4, y: 4, z: 4, core: 2. Of those that a mesh axis runs over, the one named last changes fastest.
Arguments:
- tokens: bfloat16 [65536, 4608], P(('dp', 'fsdp')), as said below
- rmsnorm_gain_vector: bfloat16 [4608], replicated, may hold values from 0.099609375 to 1.8984375
- tied_query_matrix: bfloat16 [4608, 2048], P('fsdp'), may hold values from -0.09375 to 0.09375
- adapter_down_matrix: bfloat16 [4608, 128], P('fsdp'), may hold values from -0.09375 to 0.09375
- adapter_up_matrix: bfloat16 [128, 2048], replicated, may hold values from -0.5 to 0.5
- depth: int32 [4096], P(('dp', 'fsdp')), may hold values from 1 to 3, as said below
- destination: int32 [4096], P(('dp', 'fsdp')), may hold values from 0 to 31, as said below
- cotangent: bfloat16 [32768, 2048], P(('dp', 'fsdp')), may hold values from -6 to 6
Outputs:
- query: bfloat16 [32768, 2048], P(('dp', 'fsdp'))
- grad_tokens: bfloat16 [65536, 4608], P(('dp', 'fsdp'))
- grad_down: float32 [4608, 128], replicated
- grad_up: float32 [128, 2048], replicated
Inputs may be any that keep to these rules, and one draw needn't show every extreme that they name: Blocks that stop before this recursion have depth 1; the others have depth 2 or 3. `destination`: only entries of surviving blocks are read. Each dp index is named by exactly 16 surviving blocks with its own fsdp index, and by at most 1 surviving blocks of any one device; both bounds are reached in every draw. `tokens`: float values of mixed row and feature scales.
All inputs are finite; a program needn't handle non-finite values.
Results may differ from a plain program's by a relative error of at most 0.0053.
Values may be sent and summed in bfloat16 or wider, within the bound.
No kernel may reach another device: no remote copies, remote signals or barrier semaphores. Data moves between devices by JAX's collectives and lax.ppermute only.
A program may use at most 128 MiB of HBM per device.

v0:
```python
import jax
import jax.numpy as jnp
from jax import lax
from jax.sharding import Mesh, PartitionSpec as P

DP = ("x", "y", "core")
BF16 = jnp.bfloat16
F32 = jnp.float32


def dot(a, b, dims=((1,), (0,))):
    return lax.dot_general(a, b, (dims, ((), ())), preferred_element_type=F32)


def gather_down(down):
    me = lax.axis_index("fsdp")
    rows = down.shape[0]
    full = jnp.zeros((4 * rows, down.shape[1]), down.dtype)
    for step in range(4):
        part = down
        if step:
            part = lax.ppermute(down, "fsdp", [((i + step) % 4, i) for i in range(4)])
        full = lax.dynamic_update_slice(full, part, ((me + step) % 4 * rows, 0))
    return full


def gather_weight(weight):
    chip = lax.axis_index("x") * 4 + lax.axis_index("y")
    half = weight.shape[1] // 2
    rows = weight.shape[0] // 16
    piece = lax.dynamic_slice(weight, (chip * rows, lax.axis_index("core") * half), (rows, half))
    both = lax.all_gather(piece, ("core", "fsdp", "x", "y"), axis=0, tiled=True)
    return both.reshape(2, both.shape[0] // 2, half)


def reduce_gradients(grads):
    rows, lanes = grads.shape
    parts = lax.all_to_all(grads.astype(BF16), DP, 0, 0, tiled=True)
    mine = jnp.sum(parts.reshape(32, rows // 32, lanes).astype(F32), axis=0)
    mine = lax.psum(mine, "fsdp")
    return lax.all_gather(mine, DP, axis=0, tiled=True)


def body(tokens, gain, weight, down, up, depth, destination, cotangent):
    blocks = depth.shape[0]
    rows, width = tokens.shape
    block_rows = rows // blocks
    features = cotangent.shape[1]
    capacity = cotangent.shape[0] // block_rows
    live = depth >= 2
    dest = jnp.clip(destination, 0, 31)
    hit = live[None, :] & (dest[None, :] == jnp.arange(32, dtype=jnp.int32)[:, None])
    order = jnp.arange(blocks, dtype=jnp.int32)
    source = jnp.sum(jnp.where(hit, order[None, :], 0), axis=1)
    sent = jnp.any(hit, axis=1).astype(jnp.int32)
    flags = lax.all_to_all(sent, DP, 0, 0, tiled=True)
    rank = jnp.sum(jnp.where(order[None, :] < order[:, None], flags[None, :], 0), axis=1)
    seat = jnp.clip(rank, 0, capacity - 1)
    seats = jnp.arange(capacity, dtype=jnp.int32)
    match = (flags[None, :] > 0) & (rank[None, :] == seats[:, None])
    pick = jnp.sum(jnp.where(match, order[None, :], 0), axis=1)
    full_weight = gather_weight(weight)
    full_down = gather_down(down)
    g_send = jnp.take(cotangent.reshape(capacity, block_rows, features), seat, axis=0)
    g_got = lax.all_to_all(g_send, DP, 0, 0, tiled=True)
    g = jnp.where(live[:, None, None], jnp.take(g_got, dest, axis=0), jnp.zeros((), BF16))
    g = g.reshape(rows, features)
    x = tokens.astype(F32)
    inverse = lax.rsqrt(jnp.mean(x * x, axis=-1, keepdims=True) + 1e-06)
    gain_f = gain.astype(F32)
    xn = (x * inverse * gain_f).astype(BF16)
    low = dot(xn, full_down).astype(BF16)
    dlow = dot(g, up, ((1,), (1,))).astype(BF16)
    grad_up = dot(low, g, ((0,), (0,)))
    grad_down = dot(xn, dlow, ((0,), (0,)))
    grads = jnp.concatenate([grad_down, grad_up.reshape(-1, grad_down.shape[1])], axis=0)
    grads = reduce_gradients(grads)
    grad_down, grad_up = (grads[:width], grads[width:].reshape(grad_up.shape))
    half = features // 2
    q = jnp.concatenate([dot(xn, full_weight[0]), dot(xn, full_weight[1])], axis=1)
    q = (q + dot(low, up)).astype(BF16).reshape(blocks, block_rows, features)
    q_got = lax.all_to_all(jnp.take(q, source, axis=0), DP, 0, 0, tiled=True)
    query = jnp.take(q_got, pick, axis=0).reshape(capacity * block_rows, features)
    dxn = dot(g[:, :half], full_weight[0], ((1,), (1,))) + dot(
        g[:, half:], full_weight[1], ((1,), (1,))
    )
    dxn = dxn + dot(dlow, full_down, ((1,), (1,)))
    dy = dxn * gain_f
    normed = x * inverse
    grad_tokens = inverse * (dy - normed * jnp.mean(dy * normed, axis=-1, keepdims=True))
    grad_tokens = jnp.where(jnp.repeat(live, block_rows)[:, None], grad_tokens, 0.0).astype(BF16)
    return (query, grad_tokens, grad_down, grad_up)


def solution(mesh):
    fine = Mesh(mesh.devices.reshape(4, 4, 2, 4), ("x", "y", "core", "fsdp"))
    split = P(("x", "y", "core", "fsdp"))
    in_specs = (split, P(), P("fsdp"), P("fsdp"), P(), split, split, split)
    return jax.shard_map(
        body, mesh=fine, in_specs=in_specs, out_specs=(split, split, P(), P()), check_vma=False
    )
```

profile of v0, /device:TPU:1, one launch (start us, length us, event | category | flops | bytes accessed | tf_op | source)
XLA Modules:
  0.0 356.4 jit_solution(17156562937202370914)
XLA Ops:
  7.2 4.7 %collective-permute-start = (bf16[1152,128]{1,0:T(8,128)(2,1)}, bf16[1152,128]{1,0:T(8,128)(2,1)}, u32[]{:S(2)}, u32[]{:S(2)}) collective-permute-start(bf16[1152,128]{1,0:T(8,128)(2,1)} %param.13), channel_id=1, source_target_pairs={{1,0},{2,1},{3,2},{0,3},{5,4},{6,5},{7,6},{4,7},{9,8},{10,9},{11,1... | collective-permute-start | bytes 884744 | tf_op jit(solution)/shard_map/ppermute | solution.py:22
  14.7 8.6 %all-to-all-start = ((s32[32,1,1]{2,1,0:T(1,128)}), s32[32,1,1]{2,1,0:T(1,128)S(1)}, u32[]{:S(2)}, u32[]{:S(2)}) async-start(s32[32,1,1]{2,1,0:T(1,128)} %copy.14), calls=%async_computation | async-start | bytes 32768 | tf_op jit(solution)/shard_map/all_to_all | solution.py:56
  23.4 3.3 fusion.9
  26.7 3.4 all-to-all-done
  31.7 1.6 broadcast_select_fusion.1
  33.3 4.3 %all-to-all-start.2 = ((bf16[32,16,2048]{2,1,0:T(8,128)(2,1)}), bf16[32,16,2048]{2,1,0:T(8,128)(2,1)S(1)}, u32[]{:S(2)}, u32[]{:S(2)}) async-start(bf16[32,16,2048]{2,1,0:T(8,128)(2,1)} %broadcast_select_fusion.1), calls=%async_computation.2 | async-start | bytes 4194304 | tf_op jit(solution)/shard_map/all_to_all | solution.py:65
  41.1 3.8 %convolution_convert_fusion.3 = bf16[512,128]{1,0:T(8,128)(2,1)S(1)} fusion(bf16[4608,128]{1,0:T(8,128)(2,1)S(1)} %constant_dynamic-update-slice_fusion, bf16[512,4608]{1,0:T(8,128)(2,1)} %param.10, f32[4608]{0:T(1024)S(1)} %convert_element_type.45, f32[512]{0:T(512)S(1)} %add_rsqrt_fusion), kind=kOutput, calls=%fused_computation.35 | convolution fusion | flops 613482496 | bytes 6049792 | tf_op jit(solution)/shard_map/dot_general | solution.py:12
  44.9 21.1 %all-to-all-done.2 = bf16[32,16,2048]{2,1,0:T(8,128)(2,1)S(1)} async-done(((bf16[32,16,2048]{2,1,0:T(8,128)(2,1)}), bf16[32,16,2048]{2,1,0:T(8,128)(2,1)S(1)}, u32[]{:S(2)}, u32[]{:S(2)}) %all-to-all-start.2) | async-done | bytes 2097184 | tf_op jit(solution)/shard_map/all_to_all | solution.py:65
  66.0 2.0 gather_fusion.3
  68.0 1.9 select_select_fusion
  71.4 4.1 %convolution_convert_fusion = bf16[4608,128]{1,0:T(8,128)(2,1)S(1)} fusion(bf16[512,128]{1,0:T(8,128)(2,1)S(1)} %convolution_convert_fusion.2, bf16[512,4608]{1,0:T(8,128)(2,1)} %param.10, f32[4608]{0:T(1024)S(1)} %convert_element_type.45, f32[512]{0:T(512)S(1)} %add_rsqrt_fusion), kind=kOutput, calls=%fused_computation.25 | convolution fusion | flops 614006784 | bytes 6049792 | tf_op jit(solution)/shard_map/dot_general | solution.py:12
  75.6 27.8 %all_to_all.25 = bf16[32,208,128]{2,1,0:T(8,128)(2,1)S(1)} all-to-all(bf16[32,208,128]{2,1,0:T(8,128)(2,1)S(1)} %bitcast.34), channel_id=1, replica_groups=mesh['x'=4,'y'=4,'core'=2,'fsdp'=4] {'x','y','core'}, dimensions={0} | all-to-all | bytes 3407872 | tf_op jit(solution)/shard_map/all_to_all | solution.py:38
  104.4 35.0 %all-reduce.2.cloned.1.call-done = f32[208,128]{1,0:T(8,128)} async-done(((f32[208,128]{1,0:T(8,128)}), f32[208,128]{1,0:T(8,128)}) %all-reduce.2.cloned.1.call-update) | async-done | bytes 106512 | tf_op jit(solution)/shard_map/psum | solution.py:40
  139.6 1.6 dynamic_slice.3
  141.8 48.4 %all-gather.5.cloned.1.call-done = f32[6656,128]{1,0:T(8,128)} async-done(((f32[208,128]{1,0:T(8,128)}), f32[6656,128]{1,0:T(8,128)}) %all-gather.5.cloned.1.call-update) | async-done | bytes 3407888 | tf_op jit(solution)/shard_map/all_gather | solution.py:41
  190.2 1.3 slice.41
  191.5 1.1 reshape.126
  192.6 3.2 slice.40
  195.9 81.2 %all-gather.3.cloned.1.call-done = bf16[9216,1024]{1,0:T(8,128)(2,1)} async-done(((bf16[72,1024]{1,0:T(8,128)(2,1)}), bf16[9216,1024]{1,0:T(8,128)(2,1)}) %all-gather.3.cloned.1.call-update) | async-done | bytes 18874384 | tf_op jit(solution)/shard_map/all_gather | solution.py:32
  277.0 9.2 %fusion.12 = f32[512,1024]{1,0:T(8,128)S(1)} fusion(bf16[9216,1024]{1,0:T(8,128)(2,1)} %all-gather.3.cloned.1.call-done, bf16[512,4608]{1,0:T(8,128)(2,1)} %param.10, f32[4608]{0:T(1024)S(1)} %convert_element_type.45, f32[512]{0:T(512)S(1)} %add_rsqrt_fusion), kind=kOutput, calls=%fused_computation.19 | convolution fusion | flops 4841275392 | bytes 16273408 | tf_op jit(solution)/shard_map/dot_general | solution.py:12
  286.3 1.2 copy-done.8
  287.5 7.3 %fusion.16 = f32[512,1024]{1,0:T(8,128)S(1)} fusion(bf16[9216,1024]{1,0:T(8,128)(2,1)S(1)} %copy-done.8, bf16[512,4608]{1,0:T(8,128)(2,1)} %param.10, f32[4608]{0:T(1024)S(1)} %convert_element_type.45, f32[512]{0:T(512)S(1)} %add_rsqrt_fusion), kind=kOutput, calls=%fused_computation.23 | convolution fusion | flops 4841275392 | bytes 16275456 | tf_op jit(solution)/shard_map/dot_general | solution.py:12
  294.8 2.0 fusion.18
  296.9 3.6 %gather_fusion.2 = bf16[32,16,2048]{2,1,0:T(8,128)(2,1)} fusion(bf16[32,16,2048]{2,1,0:T(8,128)(2,1)} %bitcast.33, s32[1024]{0:T(1024)S(1)} %pad_clamp_fusion.3), kind=kCustom, calls=%fused_computation.clone | custom fusion | bytes 4194432 | tf_op jit(solution)/shard_map/jit(_take)/gather | solution.py:82
  300.4 3.2 broadcast_select_fusion
  303.6 7.2 %all-to-all-start.1 = ((bf16[32,16,2048]{2,1,0:T(8,128)(2,1)}), bf16[32,16,2048]{2,1,0:T(8,128)(2,1)}, u32[]{:S(2)}, u32[]{:S(2)}) async-start(bf16[32,16,2048]{2,1,0:T(8,128)(2,1)} %broadcast_select_fusion), calls=%async_computation.1 | async-start | bytes 4194304 | tf_op jit(solution)/shard_map/all_to_all | solution.py:82
  310.8 11.4 %fusion.10 = f32[512,4608]{1,0:T(8,128)} fusion(bf16[9216,1024]{1,0:T(8,128)(2,1)} %all-gather.3.cloned.1.call-done, bf16[512,2048]{1,0:T(8,128)(2,1)S(1)} %bitcast.31), kind=kOutput, calls=%fused_computation.17 | convolution fusion | flops 4831838208 | bytes 19922944 | tf_op jit(solution)/shard_map/dot_general | solution.py:12
  322.2 11.3 %fusion.14 = f32[512,4608]{1,0:T(8,128)} fusion(bf16[9216,1024]{1,0:T(8,128)(2,1)} %all-gather.3.cloned.1.call-done, bf16[512,2048]{1,0:T(8,128)(2,1)S(1)} %bitcast.32), kind=kOutput, calls=%fused_computation.21 | convolution fusion | flops 4831838208 | bytes 19922944 | tf_op jit(solution)/shard_map/dot_general | solution.py:12
  333.5 8.1 %fusion.4 = (f32[512]{0:T(512)S(1)}, f32[512,4608]{1,0:T(8,128)S(1)}) fusion(bf16[512,4608]{1,0:T(8,128)(2,1)S(1)} %bitcast.28, f32[512]{0:T(512)S(1)} %add_rsqrt_fusion, f32[4608]{0:T(1024)S(1)} %convert_element_type.45, bf16[512,128]{1,0:T(8,128)(2,1)S(1)} %convolution_convert_fusion.2, bf16[4608,128]{1,0:T(8,128)(2,1)S(1)} %copy-done.3, ...), kind=kOutput, calls=%fused_computation.10 | convolution fusion | flops 620494336 | bytes 34363392 | tf_op jit(solution)/shard_map/dot_general | solution.py:12
  341.6 4.8 %fusion.8 = bf16[512,4608]{1,0:T(8,128)(2,1)} fusion(f32[512,4608]{1,0:T(8,128)S(1)} %get-tuple-element.8, bf16[512,4608]{1,0:T(8,128)(2,1)S(1)} %bitcast.28, f32[512]{0:T(512)S(1)} %broadcast_multiply_fusion, f32[512]{0:T(512)S(1)} %add_rsqrt_fusion, pred[512]{0:T(512)(128)(4,1)S(1)} %broadcast_in_dim.119), kind=kLoop, calls=%fused_computation.14 | loop fusion | flops 16515072 | bytes 18878976 | tf_op jit(solution)/shard_map/convert_element_type | solution.py:91
  346.5 2.2 gather_fusion
  348.7 1.2 bitcast_select_fusion
  (75 shorter events, 11.1 us)
Async XLA Ops:
  7.2 23.8 %copy-start = (bf16[256,2048]{1,0:T(8,128)(2,1)S(1)}, bf16[256,2048]{1,0:T(8,128)(2,1)}, u32[]{:S(2)}) copy-start(bf16[256,2048]{1,0:T(8,128)(2,1)} %param.17) | copy-start | bytes 3145732
  7.2 19.5 %copy-start.7 = (bf16[4608]{0:T(1024)(128)(2,1)S(1)}, bf16[4608]{0:T(1024)(128)(2,1)}, u32[]{:S(2)}) copy-start(bf16[4608]{0:T(1024)(128)(2,1)} %param.11) | copy-start | bytes 27652
  7.2 30.8 %collective-permute-start = (bf16[1152,128]{1,0:T(8,128)(2,1)}, bf16[1152,128]{1,0:T(8,128)(2,1)}, u32[]{:S(2)}, u32[]{:S(2)}) collective-permute-start(bf16[1152,128]{1,0:T(8,128)(2,1)} %param.13), channel_id=1, source_target_pairs={{1,0},{2,1},{3,2},{0,3},{5,4},{6,5},{7,6},{4,7},{9,8},{10,9},{11,1... | collective-permute-start | bytes 884744 | tf_op jit(solution)/shard_map/ppermute | solution.py:22
  11.8 27.1 %collective-permute-start.1 = (bf16[1152,128]{1,0:T(8,128)(2,1)}, bf16[1152,128]{1,0:T(8,128)(2,1)}, u32[]{:S(2)}, u32[]{:S(2)}) collective-permute-start(bf16[1152,128]{1,0:T(8,128)(2,1)} %param.13), channel_id=1, source_target_pairs={{2,0},{3,1},{0,2},{1,3},{6,4},{7,5},{4,6},{5,7},{10,8},{11,9},{8,1... | collective-permute-start | bytes 884744 | tf_op jit(solution)/shard_map/ppermute | solution.py:22
  11.9 28.1 %collective-permute-start.2 = (bf16[1152,128]{1,0:T(8,128)(2,1)}, bf16[1152,128]{1,0:T(8,128)(2,1)S(1)}, u32[]{:S(2)}, u32[]{:S(2)}) collective-permute-start(bf16[1152,128]{1,0:T(8,128)(2,1)} %param.13), channel_id=1, source_target_pairs={{3,0},{0,1},{1,2},{2,3},{7,4},{4,5},{5,6},{6,7},{11,8},{8,9},{9,10... | collective-permute-start | bytes 884744 | tf_op jit(solution)/shard_map/ppermute | solution.py:22
  14.7 15.5 %all-to-all-start = ((s32[32,1,1]{2,1,0:T(1,128)}), s32[32,1,1]{2,1,0:T(1,128)S(1)}, u32[]{:S(2)}, u32[]{:S(2)}) async-start(s32[32,1,1]{2,1,0:T(1,128)} %copy.14), calls=%async_computation | async-start | bytes 32768 | tf_op jit(solution)/shard_map/all_to_all | solution.py:56
  31.7 6.2 %copy-start.6 = (bf16[1152,128]{1,0:T(8,128)(2,1)S(1)}, bf16[1152,128]{1,0:T(8,128)(2,1)}, u32[]{:S(2)}) copy-start(bf16[1152,128]{1,0:T(8,128)(2,1)} %param.13) | copy-start | bytes 884740
  31.7 6.2 %copy-start.9 = (s32[32]{0:T(128)S(1)}, s32[32]{0:T(128)}, u32[]{:S(2)}) copy-start(s32[32]{0:T(128)} %param.16) | copy-start | bytes 388
  33.3 32.7 %all-to-all-start.2 = ((bf16[32,16,2048]{2,1,0:T(8,128)(2,1)}), bf16[32,16,2048]{2,1,0:T(8,128)(2,1)S(1)}, u32[]{:S(2)}, u32[]{:S(2)}) async-start(bf16[32,16,2048]{2,1,0:T(8,128)(2,1)} %broadcast_select_fusion.1), calls=%async_computation.2 | async-start | bytes 4194304 | tf_op jit(solution)/shard_map/all_to_all | solution.py:65
  37.6 101.7 %all-reduce.2.cloned.1.call-start = ((), (), s32[]{:S(2)}) async-start(), calls=%async_computation.5 | async-start | bytes 212992 | tf_op jit(solution)/shard_map/psum | solution.py:40
  40.0 1.0 copy-start.2
  44.8 25.1 %copy-start.4 = (bf16[128,2048]{1,0:T(8,128)(2,1)S(1)}, bf16[128,2048]{1,0:T(8,128)(2,1)}, u32[]{:S(2)}) copy-start(bf16[128,2048]{1,0:T(8,128)(2,1)} %param.14) | copy-start | bytes 1572868
  104.3 85.9 %all-gather.5.cloned.1.call-start = ((), (), s32[]{:S(2)}) async-start(), calls=%async_computation.6 | async-start | bytes 3514368 | tf_op jit(solution)/shard_map/all_gather | solution.py:41
  139.3 137.7 %all-gather.3.cloned.1.call-start = ((), (), s32[]{:S(2)}) async-start(), calls=%async_computation.4 | async-start | bytes 19021824 | tf_op jit(solution)/shard_map/all_gather | solution.py:32
  277.0 10.5 %copy-start.8 = (bf16[9216,1024]{1,0:T(8,128)(2,1)S(1)}, bf16[9216,1024]{1,0:T(8,128)(2,1)}, u32[]{:S(2)}) copy-start(bf16[9216,1024]{1,0:T(8,128)(2,1)} %all-gather.3.cloned.1.call-done) | copy-start | bytes 56623108
  287.5 7.3 %copy-start.5 = (bf16[128,2048]{1,0:T(8,128)(2,1)S(1)}, bf16[128,2048]{1,0:T(8,128)(2,1)}, u32[]{:S(2)}) copy-start(bf16[128,2048]{1,0:T(8,128)(2,1)} %param.14) | copy-start | bytes 1572868
  303.6 42.9 %all-to-all-start.1 = ((bf16[32,16,2048]{2,1,0:T(8,128)(2,1)}), bf16[32,16,2048]{2,1,0:T(8,128)(2,1)}, u32[]{:S(2)}, u32[]{:S(2)}) async-start(bf16[32,16,2048]{2,1,0:T(8,128)(2,1)} %broadcast_select_fusion), calls=%async_computation.1 | async-start | bytes 4194304 | tf_op jit(solution)/shard_map/all_to_all | solution.py:82
  310.8 22.7 %slice-start = ((s8[4718592]{0:T(1024)(128)(4,1)}), s8[4194304]{0:T(1024)(128)(4,1)S(1)}, s32[]{:S(2)}) async-start(s8[4718592]{0:T(1024)(128)(4,1)} %bitcast.27), calls=%async_computation.7 | async-start | bytes 8388608
  322.2 11.3 %slice-start.1 = ((s8[4718592]{0:T(1024)(128)(4,1)}), s8[524288]{0:T(1024)(128)(4,1)S(1)}, s32[]{:S(2)}) async-start(s8[4718592]{0:T(1024)(128)(4,1)} %bitcast.27), calls=%async_computation.8 | async-start | bytes 1048576
  322.2 11.3 %copy-start.3 = (bf16[4608,128]{1,0:T(8,128)(2,1)S(1)}, bf16[4608,128]{1,0:T(8,128)(2,1)}, u32[]{:S(2)}) copy-start(bf16[4608,128]{1,0:T(8,128)(2,1)} %copy-done.2) | copy-start | bytes 3538948
  341.6 8.2 %copy-start.1 = (bf16[256,2048]{1,0:T(8,128)(2,1)S(1)}, bf16[256,2048]{1,0:T(8,128)(2,1)}, u32[]{:S(2)}) copy-start(bf16[256,2048]{1,0:T(8,128)(2,1)} %param.17) | copy-start | bytes 3145732
Sparse Core Ops, SparseCore 0:
  104.4 34.8 all-reduce.1
  141.8 48.3 all-gather.4
  194.2 82.7 all-gather.2
where the time goes:
time: 357 us; the launch traced here: 356 us
  waiting for transfers between devices  189 us (53%)
  matrix products  58.4 us (16%)
  blocking collectives  27.8 us (8%)
  starting transfers between devices  25.7 us (7%)
  local copies, waits for them, and re-layouts  21.6 us (6%)
  other arithmetic  19.5 us (5%)
  between operations  14.2 us (4%)
    all_gather x1, waiting for transfers between devices, gather_weight(): both = lax.all_gather(piece, ('core', 'fsdp', 'x', 'y'), axis=0, tiled=True)  81.2 us
    dot_general x10, matrix products, dot(): return lax.dot_general(a, b, (dims, ((), ())), preferred_element_type=F32)  58.4 us
    all_gather x1, waiting for transfers between devices, reduce_gradients(): return lax.all_gather(mine, DP, axis=0, tiled=True)  48.4 us
    psum x1, waiting for transfers between devices, reduce_gradients(): mine = lax.psum(mine, 'fsdp')  35 us
    all_to_all x1, blocking collectives, reduce_gradients(): parts = lax.all_to_all(grads.astype(BF16), DP, 0, 0, tiled=True)  27.8 us
    all_to_all x1, waiting for transfers between devices, body(): g_got = lax.all_to_all(g_send, DP, 0, 0, tiled=True)  21.1 us
    all_to_all x1, starting transfers between devices, body(): flags = lax.all_to_all(sent, DP, 0, 0, tiled=True)  8.6 us
    all_to_all x1, starting transfers between devices, body(): q_got = lax.all_to_all(jnp.take(q, source, axis=0), DP, 0, 0, tiled=True)  7.17 us
  transfers between devices with their start and end apart: 9, of which 5 were waited for; matrix products, arithmetic and copies ran while one was open for 16% of the time, Pallas kernels for 0%

commit v1 on v0

--- a/solution.py
+++ b/solution.py
@@ -38,7 +38,7 @@
     parts = lax.all_to_all(grads.astype(BF16), DP, 0, 0, tiled=True)
     mine = jnp.sum(parts.reshape(32, rows // 32, lanes).astype(F32), axis=0)
     mine = lax.psum(mine, "fsdp")
-    return lax.all_gather(mine, DP, axis=0, tiled=True)
+    return jnp.concatenate(lax.all_to_all(jnp.stack([mine] * lax.axis_size(DP)), DP, 0, 0), axis=0)
 
 
 def body(tokens, gain, weight, down, up, depth, destination, cotangent):

time: 357 us -> 304 us (0.85)
  waiting for transfers between devices: 189 us -> 123 us
  starting transfers between devices: 25.7 us -> 34 us
    all_gather x1, waiting for transfers between devices: 81.2 us -> 0.01 us  [gather_weight(): both = lax.all_gather(piece, ('core', 'fsdp', 'x', 'y'), axis=0, tiled=True)]
    all_to_all x0 -> x1, waiting for transfers between devices: none -> 65.5 us  [reduce_gradients(): lax.all_to_all(jnp.stack([mine] * lax.axis_size(DP)), DP, 0, 0)]
    all_gather x1 -> x0, waiting for transfers between devices: 48.4 us -> none  [reduce_gradients(): return lax.all_gather(mine, DP, axis=0, tiled=True)]
    all_to_all x0 -> x1, starting transfers between devices: none -> 10.3 us  [reduce_gradients(): lax.all_to_all(jnp.stack([mine] * lax.axis_size(DP)), DP, 0, 0)]
  transfers between devices with their start and end apart: 9 -> 9, of which waited for: 5 -> 4; matrix products, arithmetic and copies ran while one was open for 16% -> 20% of each run, Pallas kernels for 0% -> 0%
where the time goes in v1:
time: 304 us
  waiting for transfers between devices  123 us (40%)
  matrix products  58.4 us (19%)
  starting transfers between devices  34 us (11%)
  blocking collectives  27.8 us (9%)
  local copies, waits for them, and re-layouts  24.4 us (8%)
  other arithmetic  19.5 us (6%)
  between operations  16 us (5%)
    all_to_all x1, waiting for transfers between devices, reduce_gradients(): lax.all_to_all(jnp.stack([mine] * lax.axis_size(DP)), DP, 0, 0)  65.5 us
    dot_general x10, matrix products, dot(): return lax.dot_general(a, b, (dims, ((), ())), preferred_element_type=F32)  58.4 us
    psum x1, waiting for transfers between devices, reduce_gradients(): mine = lax.psum(mine, 'fsdp')  33.3 us
    all_to_all x1, blocking collectives, reduce_gradients(): parts = lax.all_to_all(grads.astype(BF16), DP, 0, 0, tiled=True)  27.8 us
    all_to_all x1, waiting for transfers between devices, body(): g_got = lax.all_to_all(g_send, DP, 0, 0, tiled=True)  21.1 us
    all_to_all x1, starting transfers between devices, reduce_gradients(): lax.all_to_all(jnp.stack([mine] * lax.axis_size(DP)), DP, 0, 0)  10.3 us
    all_to_all x1, starting transfers between devices, body(): flags = lax.all_to_all(sent, DP, 0, 0, tiled=True)  8.6 us
  transfers between devices with their start and end apart: 9, of which 4 were waited for; matrix products, arithmetic and copies ran while one was open for 20% of the time, Pallas kernels for 0%

profile of v1, /device:TPU:1, one launch (start us, length us, event | category | flops | bytes accessed | tf_op | source)
XLA Modules:
  0.0 303.6 jit_solution(13751810822933519023)
XLA Ops:
  8.0 4.7 %collective-permute-start = (bf16[1152,128]{1,0:T(8,128)(2,1)}, bf16[1152,128]{1,0:T(8,128)(2,1)}, u32[]{:S(2)}, u32[]{:S(2)}) collective-permute-start(bf16[1152,128]{1,0:T(8,128)(2,1)} %param.13), channel_id=1, source_target_pairs={{1,0},{2,1},{3,2},{0,3},{5,4},{6,5},{7,6},{4,7},{9,8},{10,9},{11,1... | collective-permute-start | bytes 884744 | tf_op jit(solution)/shard_map/ppermute | solution.py:22
  15.5 8.6 %all-to-all-start = ((s32[32,1,1]{2,1,0:T(1,128)}), s32[32,1,1]{2,1,0:T(1,128)S(1)}, u32[]{:S(2)}, u32[]{:S(2)}) async-start(s32[32,1,1]{2,1,0:T(1,128)} %copy.14), calls=%async_computation | async-start | bytes 32768 | tf_op jit(solution)/shard_map/all_to_all | solution.py:56
  24.2 3.3 %fusion.9 = f32[512]{0:T(512)S(1)} fusion(bf16[512,4608]{1,0:T(8,128)(2,1)} %param.10), kind=kLoop, calls=%fused_computation.15 | loop fusion | flops 7077376 | bytes 4720640 | tf_op jit(solution)/shard_map/reduce_sum | solution.py:69
  27.6 3.4 %all-to-all-done = s32[32,1,1]{2,1,0:T(1,128)S(1)} async-done(((s32[32,1,1]{2,1,0:T(1,128)}), s32[32,1,1]{2,1,0:T(1,128)S(1)}, u32[]{:S(2)}, u32[]{:S(2)}) %all-to-all-start) | async-done | bytes 160 | tf_op jit(solution)/shard_map/all_to_all | solution.py:56
  32.5 1.6 broadcast_select_fusion.1
  34.1 4.3 %all-to-all-start.2 = ((bf16[32,16,2048]{2,1,0:T(8,128)(2,1)}), bf16[32,16,2048]{2,1,0:T(8,128)(2,1)S(1)}, u32[]{:S(2)}, u32[]{:S(2)}) async-start(bf16[32,16,2048]{2,1,0:T(8,128)(2,1)} %broadcast_select_fusion.1), calls=%async_computation.2 | async-start | bytes 4194304 | tf_op jit(solution)/shard_map/all_to_all | solution.py:65
  41.9 3.8 %convolution_convert_fusion.3 = bf16[512,128]{1,0:T(8,128)(2,1)S(1)} fusion(bf16[4608,128]{1,0:T(8,128)(2,1)S(1)} %constant_dynamic-update-slice_fusion, bf16[512,4608]{1,0:T(8,128)(2,1)} %param.10, f32[4608]{0:T(1024)S(1)} %convert_element_type.45, f32[512]{0:T(512)S(1)} %add_rsqrt_fusion), kind=kOutput, calls=%fused_computation.35 | convolution fusion | flops 613482496 | bytes 6049792 | tf_op jit(solution)/shard_map/dot_general | solution.py:12
  45.7 21.1 %all-to-all-done.2 = bf16[32,16,2048]{2,1,0:T(8,128)(2,1)S(1)} async-done(((bf16[32,16,2048]{2,1,0:T(8,128)(2,1)}), bf16[32,16,2048]{2,1,0:T(8,128)(2,1)S(1)}, u32[]{:S(2)}, u32[]{:S(2)}) %all-to-all-start.2) | async-done | bytes 2097184 | tf_op jit(solution)/shard_map/all_to_all | solution.py:65
  66.8 2.0 gather_fusion.3
  68.8 1.9 select_select_fusion
  72.2 4.1 %convolution_convert_fusion = bf16[4608,128]{1,0:T(8,128)(2,1)S(1)} fusion(bf16[512,128]{1,0:T(8,128)(2,1)S(1)} %convolution_convert_fusion.2, bf16[512,4608]{1,0:T(8,128)(2,1)} %param.10, f32[4608]{0:T(1024)S(1)} %convert_element_type.45, f32[512]{0:T(512)S(1)} %add_rsqrt_fusion), kind=kOutput, calls=%fused_computation.25 | convolution fusion | flops 614006784 | bytes 6049792 | tf_op jit(solution)/shard_map/dot_general | solution.py:12
  76.4 27.8 %all_to_all.30 = bf16[32,208,128]{2,1,0:T(8,128)(2,1)S(1)} all-to-all(bf16[32,208,128]{2,1,0:T(8,128)(2,1)S(1)} %bitcast.35), channel_id=1, replica_groups=mesh['x'=4,'y'=4,'core'=2,'fsdp'=4] {'x','y','core'}, dimensions={0} | all-to-all | bytes 3407872 | tf_op jit(solution)/shard_map/all_to_all | solution.py:38
  105.2 1.6 dynamic_slice.3
  106.8 33.3 %all-reduce.2.cloned.1.call-done = f32[208,128]{1,0:T(8,128)} async-done(((f32[208,128]{1,0:T(8,128)}), f32[208,128]{1,0:T(8,128)}) %all-reduce.2.cloned.1.call-update) | async-done | bytes 106512 | tf_op jit(solution)/shard_map/psum | solution.py:40
  140.2 2.9 stack.2
  143.0 10.3 %all-to-all-start.4 = ((f32[32,208,128]{2,1,0:T(8,128)}), f32[32,208,128]{2,1,0:T(8,128)}, u32[]{:S(2)}, u32[]{:S(2)}) async-start(f32[32,208,128]{2,1,0:T(8,128)} %stack.2), calls=%async_computation.4 | async-start | bytes 6815744 | tf_op jit(solution)/shard_map/all_to_all | solution.py:41
  153.9 65.5 %all-to-all-done.4 = f32[32,208,128]{2,1,0:T(8,128)} async-done(((f32[32,208,128]{2,1,0:T(8,128)}), f32[32,208,128]{2,1,0:T(8,128)}, u32[]{:S(2)}, u32[]{:S(2)}) %all-to-all-start.4) | async-done | bytes 3407904 | tf_op jit(solution)/shard_map/all_to_all | solution.py:41
  219.4 3.3 %slice.40 = f32[4608,128]{1,0:T(8,128)} slice(f32[6656,128]{1,0:T(8,128)} %bitcast.10), slice={[0:4608], [0:128]} | slice | bytes 4718592 | tf_op jit(solution)/shard_map/slice | solution.py:78
  222.7 1.3 slice.41
  225.1 9.2 %fusion.12 = f32[512,1024]{1,0:T(8,128)S(1)} fusion(bf16[9216,1024]{1,0:T(8,128)(2,1)} %all-gather.2.cloned.1.call-done, bf16[512,4608]{1,0:T(8,128)(2,1)} %param.10, f32[4608]{0:T(1024)S(1)} %convert_element_type.45, f32[512]{0:T(512)S(1)} %add_rsqrt_fusion), kind=kOutput, calls=%fused_computation.19 | convolution fusion | flops 4841275392 | bytes 16273408 | tf_op jit(solution)/shard_map/dot_general | solution.py:12
  234.3 1.2 copy-done.8
  235.6 7.3 %fusion.16 = f32[512,1024]{1,0:T(8,128)S(1)} fusion(bf16[9216,1024]{1,0:T(8,128)(2,1)S(1)} %copy-done.8, bf16[512,4608]{1,0:T(8,128)(2,1)} %param.10, f32[4608]{0:T(1024)S(1)} %convert_element_type.45, f32[512]{0:T(512)S(1)} %add_rsqrt_fusion), kind=kOutput, calls=%fused_computation.23 | convolution fusion | flops 4841275392 | bytes 16275456 | tf_op jit(solution)/shard_map/dot_general | solution.py:12
  242.9 2.0 fusion.18
  244.9 3.6 %gather_fusion.2 = bf16[32,16,2048]{2,1,0:T(8,128)(2,1)} fusion(bf16[32,16,2048]{2,1,0:T(8,128)(2,1)} %bitcast.34, s32[1024]{0:T(1024)S(1)} %pad_clamp_fusion.3), kind=kCustom, calls=%fused_computation.clone | custom fusion | bytes 4194432 | tf_op jit(solution)/shard_map/jit(_take)/gather | solution.py:82
  248.5 3.2 %broadcast_select_fusion = bf16[32,16,2048]{2,1,0:T(8,128)(2,1)} fusion(bf16[32,16,2048]{2,1,0:T(8,128)(2,1)} %gather_fusion.2, pred[32]{0:T(512)(128)(4,1)S(1)} %compare_and_fusion.1), kind=kLoop, calls=%fused_computation.31 | loop fusion | flops 1048576 | bytes 4194336 | tf_op jit(solution)/shard_map/jit(_take)/select_n | solution.py:82
  251.7 5.4 %all-to-all-start.1 = ((bf16[32,16,2048]{2,1,0:T(8,128)(2,1)}), bf16[32,16,2048]{2,1,0:T(8,128)(2,1)}, u32[]{:S(2)}, u32[]{:S(2)}) async-start(bf16[32,16,2048]{2,1,0:T(8,128)(2,1)} %broadcast_select_fusion), calls=%async_computation.1 | async-start | bytes 4194304 | tf_op jit(solution)/shard_map/all_to_all | solution.py:82
  257.1 11.3 %fusion.10 = f32[512,4608]{1,0:T(8,128)} fusion(bf16[9216,1024]{1,0:T(8,128)(2,1)} %all-gather.2.cloned.1.call-done, bf16[512,2048]{1,0:T(8,128)(2,1)S(1)} %bitcast.32), kind=kOutput, calls=%fused_computation.17 | convolution fusion | flops 4831838208 | bytes 19922944 | tf_op jit(solution)/shard_map/dot_general | solution.py:12
  268.5 11.3 %fusion.14 = f32[512,4608]{1,0:T(8,128)} fusion(bf16[9216,1024]{1,0:T(8,128)(2,1)} %all-gather.2.cloned.1.call-done, bf16[512,2048]{1,0:T(8,128)(2,1)S(1)} %bitcast.33), kind=kOutput, calls=%fused_computation.21 | convolution fusion | flops 4831838208 | bytes 19922944 | tf_op jit(solution)/shard_map/dot_general | solution.py:12
  279.9 8.1 %fusion.4 = (f32[512]{0:T(512)S(1)}, f32[512,4608]{1,0:T(8,128)S(1)}) fusion(bf16[512,4608]{1,0:T(8,128)(2,1)S(1)} %bitcast.29, f32[512]{0:T(512)S(1)} %add_rsqrt_fusion, f32[4608]{0:T(1024)S(1)} %convert_element_type.45, bf16[512,128]{1,0:T(8,128)(2,1)S(1)} %convolution_convert_fusion.2, bf16[4608,128]{1,0:T(8,128)(2,1)S(1)} %copy-done.3, ...), kind=kOutput, calls=%fused_computation.10 | convolution fusion | flops 620494336 | bytes 34363392 | tf_op jit(solution)/shard_map/dot_general | solution.py:12
  288.0 4.8 %fusion.8 = bf16[512,4608]{1,0:T(8,128)(2,1)} fusion(f32[512,4608]{1,0:T(8,128)S(1)} %get-tuple-element.8, bf16[512,4608]{1,0:T(8,128)(2,1)S(1)} %bitcast.29, f32[512]{0:T(512)S(1)} %broadcast_multiply_fusion, f32[512]{0:T(512)S(1)} %add_rsqrt_fusion, pred[512]{0:T(512)(128)(4,1)S(1)} %broadcast_in_dim.119), kind=kLoop, calls=%fused_computation.14 | loop fusion | flops 16515072 | bytes 18878976 | tf_op jit(solution)/shard_map/convert_element_type | solution.py:91
  292.8 2.2 gather_fusion
  295.0 1.2 bitcast_select_fusion
  (75 shorter events, 12.0 us)
Async XLA Ops:
  8.0 23.8 %copy-start = (bf16[256,2048]{1,0:T(8,128)(2,1)S(1)}, bf16[256,2048]{1,0:T(8,128)(2,1)}, u32[]{:S(2)}) copy-start(bf16[256,2048]{1,0:T(8,128)(2,1)} %param.17) | copy-start | bytes 3145732
  8.0 19.5 %copy-start.7 = (bf16[4608]{0:T(1024)(128)(2,1)S(1)}, bf16[4608]{0:T(1024)(128)(2,1)}, u32[]{:S(2)}) copy-start(bf16[4608]{0:T(1024)(128)(2,1)} %param.11) | copy-start | bytes 27652
  8.0 30.8 %collective-permute-start = (bf16[1152,128]{1,0:T(8,128)(2,1)}, bf16[1152,128]{1,0:T(8,128)(2,1)}, u32[]{:S(2)}, u32[]{:S(2)}) collective-permute-start(bf16[1152,128]{1,0:T(8,128)(2,1)} %param.13), channel_id=1, source_target_pairs={{1,0},{2,1},{3,2},{0,3},{5,4},{6,5},{7,6},{4,7},{9,8},{10,9},{11,1... | collective-permute-start | bytes 884744 | tf_op jit(solution)/shard_map/ppermute | solution.py:22
  12.7 27.1 %collective-permute-start.1 = (bf16[1152,128]{1,0:T(8,128)(2,1)}, bf16[1152,128]{1,0:T(8,128)(2,1)}, u32[]{:S(2)}, u32[]{:S(2)}) collective-permute-start(bf16[1152,128]{1,0:T(8,128)(2,1)} %param.13), channel_id=1, source_target_pairs={{2,0},{3,1},{0,2},{1,3},{6,4},{7,5},{4,6},{5,7},{10,8},{11,9},{8,1... | collective-permute-start | bytes 884744 | tf_op jit(solution)/shard_map/ppermute | solution.py:22
  12.7 28.1 %collective-permute-start.2 = (bf16[1152,128]{1,0:T(8,128)(2,1)}, bf16[1152,128]{1,0:T(8,128)(2,1)S(1)}, u32[]{:S(2)}, u32[]{:S(2)}) collective-permute-start(bf16[1152,128]{1,0:T(8,128)(2,1)} %param.13), channel_id=1, source_target_pairs={{3,0},{0,1},{1,2},{2,3},{7,4},{4,5},{5,6},{6,7},{11,8},{8,9},{9,10... | collective-permute-start | bytes 884744 | tf_op jit(solution)/shard_map/ppermute | solution.py:22
  15.5 15.5 %all-to-all-start = ((s32[32,1,1]{2,1,0:T(1,128)}), s32[32,1,1]{2,1,0:T(1,128)S(1)}, u32[]{:S(2)}, u32[]{:S(2)}) async-start(s32[32,1,1]{2,1,0:T(1,128)} %copy.14), calls=%async_computation | async-start | bytes 32768 | tf_op jit(solution)/shard_map/all_to_all | solution.py:56
  32.5 6.2 %copy-start.6 = (bf16[1152,128]{1,0:T(8,128)(2,1)S(1)}, bf16[1152,128]{1,0:T(8,128)(2,1)}, u32[]{:S(2)}) copy-start(bf16[1152,128]{1,0:T(8,128)(2,1)} %param.13) | copy-start | bytes 884740
  32.5 6.2 %copy-start.9 = (s32[32]{0:T(128)S(1)}, s32[32]{0:T(128)}, u32[]{:S(2)}) copy-start(s32[32]{0:T(128)} %param.16) | copy-start | bytes 388
  34.1 32.7 %all-to-all-start.2 = ((bf16[32,16,2048]{2,1,0:T(8,128)(2,1)}), bf16[32,16,2048]{2,1,0:T(8,128)(2,1)S(1)}, u32[]{:S(2)}, u32[]{:S(2)}) async-start(bf16[32,16,2048]{2,1,0:T(8,128)(2,1)} %broadcast_select_fusion.1), calls=%async_computation.2 | async-start | bytes 4194304 | tf_op jit(solution)/shard_map/all_to_all | solution.py:65
  38.4 101.7 %all-reduce.2.cloned.1.call-start = ((), (), s32[]{:S(2)}) async-start(), calls=%async_computation.6 | async-start | bytes 212992 | tf_op jit(solution)/shard_map/psum | solution.py:40
  40.9 1.0 copy-start.2
  45.7 25.1 %copy-start.4 = (bf16[128,2048]{1,0:T(8,128)(2,1)S(1)}, bf16[128,2048]{1,0:T(8,128)(2,1)}, u32[]{:S(2)}) copy-start(bf16[128,2048]{1,0:T(8,128)(2,1)} %param.14) | copy-start | bytes 1572868
  105.1 120.0 %all-gather.2.cloned.1.call-start = ((), (), s32[]{:S(2)}) async-start(), calls=%async_computation.5 | async-start | bytes 19021824 | tf_op jit(solution)/shard_map/all_gather | solution.py:32
  143.0 76.4 %all-to-all-start.4 = ((f32[32,208,128]{2,1,0:T(8,128)}), f32[32,208,128]{2,1,0:T(8,128)}, u32[]{:S(2)}, u32[]{:S(2)}) async-start(f32[32,208,128]{2,1,0:T(8,128)} %stack.2), calls=%async_computation.4 | async-start | bytes 6815744 | tf_op jit(solution)/shard_map/all_to_all | solution.py:41
  225.1 10.5 %copy-start.8 = (bf16[9216,1024]{1,0:T(8,128)(2,1)S(1)}, bf16[9216,1024]{1,0:T(8,128)(2,1)}, u32[]{:S(2)}) copy-start(bf16[9216,1024]{1,0:T(8,128)(2,1)} %all-gather.2.cloned.1.call-done) | copy-start | bytes 56623108
  235.6 7.3 %copy-start.5 = (bf16[128,2048]{1,0:T(8,128)(2,1)S(1)}, bf16[128,2048]{1,0:T(8,128)(2,1)}, u32[]{:S(2)}) copy-start(bf16[128,2048]{1,0:T(8,128)(2,1)} %param.14) | copy-start | bytes 1572868
  251.7 41.1 %all-to-all-start.1 = ((bf16[32,16,2048]{2,1,0:T(8,128)(2,1)}), bf16[32,16,2048]{2,1,0:T(8,128)(2,1)}, u32[]{:S(2)}, u32[]{:S(2)}) async-start(bf16[32,16,2048]{2,1,0:T(8,128)(2,1)} %broadcast_select_fusion), calls=%async_computation.1 | async-start | bytes 4194304 | tf_op jit(solution)/shard_map/all_to_all | solution.py:82
  257.1 22.7 %slice-start = ((s8[4718592]{0:T(1024)(128)(4,1)}), s8[4194304]{0:T(1024)(128)(4,1)S(1)}, s32[]{:S(2)}) async-start(s8[4718592]{0:T(1024)(128)(4,1)} %bitcast.28), calls=%async_computation.7 | async-start | bytes 8388608
  268.5 11.4 %slice-start.1 = ((s8[4718592]{0:T(1024)(128)(4,1)}), s8[524288]{0:T(1024)(128)(4,1)S(1)}, s32[]{:S(2)}) async-start(s8[4718592]{0:T(1024)(128)(4,1)} %bitcast.28), calls=%async_computation.8 | async-start | bytes 1048576
  268.5 11.4 %copy-start.3 = (bf16[4608,128]{1,0:T(8,128)(2,1)S(1)}, bf16[4608,128]{1,0:T(8,128)(2,1)}, u32[]{:S(2)}) copy-start(bf16[4608,128]{1,0:T(8,128)(2,1)} %copy-done.2) | copy-start | bytes 3538948
  288.0 8.2 %copy-start.1 = (bf16[256,2048]{1,0:T(8,128)(2,1)S(1)}, bf16[256,2048]{1,0:T(8,128)(2,1)}, u32[]{:S(2)}) copy-start(bf16[256,2048]{1,0:T(8,128)(2,1)} %param.17) | copy-start | bytes 3145732
Sparse Core Ops, SparseCore 0:
  105.3 34.8 all-reduce.1
Sparse Core Ops, SparseCore 1:
  109.2 111.6 all-gather.1
